TPU v7x, 256 devices: a whole 4x4x8 slice. The times are simulated.
256 devices in a mesh: row: 32 (over y_hi, z, core), ch: 8 (over y_lo, x).
Axes of the slice: x: 4, y: 4 (y_hi: 2, y_lo: 2; y = y_hi * 2 + y_lo), z: 8, core: 2. Of those that a mesh axis runs over, the one named last changes fastest.
Arguments:
- pair_act: bfloat16 [512, 512, 128], P('row', 'ch'), may hold values from -240 to 240
- cotangent: bfloat16 [512, 512, 128], P('row', 'ch'), may hold values from -6 to 6
- in_gain: float32 [128], replicated, may hold values from 0.25 to 1.75
- in_bias: float32 [128], replicated, may hold values from -3 to 3
- proj_weight: bfloat16 [128, 640], replicated, may hold values from -0.5 to 0.5
- out_gain: float32 [128], replicated, may hold values from 0.25 to 1.75
- out_bias: float32 [128], replicated, may hold values from -3 to 3
- out_weight: bfloat16 [128, 128], replicated, may hold values from -0.5 to 0.5
Outputs:
- grad_pair: bfloat16 [512, 512, 128], P('row', 'ch')
All inputs are finite; a program needn't handle non-finite values.
Results may differ from a plain program's by a relative error of at most 0.0072.
Values may be sent and summed in bfloat16 or wider, within the bound.
A program may use at most 64 MiB of HBM per device.

v0:
```python
import jax
import jax.numpy as jnp
from jax import lax
from jax.sharding import PartitionSpec as P

EPSILON = 1e-05


def normalize(values, axis):
    center = jnp.mean(values, axis=axis, keepdims=True)
    shifted = values - center
    scale_inv = lax.rsqrt(jnp.mean(shifted * shifted, axis=axis, keepdims=True) + EPSILON)
    return (shifted * scale_inv, scale_inv)


def norm_back(grad_hat, normed, scale_inv, axis):
    first = jnp.mean(grad_hat, axis=axis, keepdims=True)
    second = jnp.mean(grad_hat * normed, axis=axis, keepdims=True)
    return scale_inv * (grad_hat - first - normed * second)


def on_device(pair_act, cotangent, in_gain, in_bias, proj_weight, out_gain, out_bias, out_weight):
    rows_here, cols_here, width = pair_act.shape
    flat = pair_act.astype(jnp.float32).reshape(rows_here * cols_here, width)
    normed, scale_inv = normalize(flat, -1)
    normal_in = (normed * in_gain + in_bias).astype(jnp.bfloat16)
    projected = jnp.einsum("pd,de->ep", normal_in, proj_weight, preferred_element_type=jnp.float32)
    blocks = jnp.split(projected, 5, axis=0)
    left_sig = jax.nn.sigmoid(blocks[1])
    right_sig = jax.nn.sigmoid(blocks[3])
    left_fac = (left_sig * blocks[0]).astype(jnp.bfloat16).reshape(width, rows_here, cols_here)
    right_fac = (right_sig * blocks[2]).astype(jnp.bfloat16).reshape(width, rows_here, cols_here)
    left_chan, right_chan = (
        lax.all_to_all(left_fac, "ch", split_axis=0, concat_axis=2, tiled=True),
        lax.all_to_all(right_fac, "ch", split_axis=0, concat_axis=2, tiled=True),
    )
    tri_chan = jnp.einsum(
        "cik,cjk->cij",
        left_chan,
        lax.all_gather(right_chan, "row", axis=1, tiled=True),
        preferred_element_type=jnp.float32,
    ).astype(jnp.bfloat16)
    tri_back = lax.all_to_all(tri_chan, "ch", split_axis=2, concat_axis=0, tiled=True)
    tri_hat, tri_inv = normalize(tri_back.astype(jnp.float32).reshape(width, -1), 0)
    normal_out = (tri_hat * out_gain[:, None] + out_bias[:, None]).astype(jnp.bfloat16)
    mixed = jnp.einsum("cp,ce->ep", normal_out, out_weight, preferred_element_type=jnp.float32)
    out_gate = jax.nn.sigmoid(blocks[4])
    grad_out = cotangent.astype(jnp.float32).reshape(rows_here * cols_here, width).T
    grad_mixed = (grad_out * out_gate).astype(jnp.bfloat16)
    grad_logit = grad_out * mixed * out_gate * (1.0 - out_gate)
    grad_normal = jnp.einsum(
        "ep,ce->cp", grad_mixed, out_weight, preferred_element_type=jnp.float32
    )
    grad_tri = norm_back(grad_normal * out_gain[:, None], tri_hat, tri_inv, 0)
    grad_tri = grad_tri.astype(jnp.bfloat16).reshape(width, rows_here, cols_here)
    grad_chan = lax.all_to_all(grad_tri, "ch", split_axis=0, concat_axis=2, tiled=True)
    grad_cols = lax.all_to_all(grad_chan, "row", split_axis=2, concat_axis=1, tiled=True)
    block = grad_chan
    grad_left = jnp.einsum(
        "cij,cjk->cik",
        block,
        lax.all_gather(right_chan, "row", axis=1, tiled=True),
        preferred_element_type=jnp.float32,
    )
    block = grad_cols
    grad_right = jnp.einsum(
        "cij,cik->cjk",
        block,
        lax.all_gather(left_chan, "row", axis=1, tiled=True),
        preferred_element_type=jnp.float32,
    )
    left_back, right_back = (
        lax.all_to_all(
            grad_left.astype(jnp.bfloat16), "ch", split_axis=2, concat_axis=0, tiled=True
        ),
        lax.all_to_all(
            grad_right.astype(jnp.bfloat16), "ch", split_axis=2, concat_axis=0, tiled=True
        ),
    )
    left_grad = left_back.astype(jnp.float32).reshape(width, -1)
    right_grad = right_back.astype(jnp.float32).reshape(width, -1)
    grad_proj = jnp.concatenate(
        [
            left_grad * left_sig,
            left_grad * blocks[0] * left_sig * (1.0 - left_sig),
            right_grad * right_sig,
            right_grad * blocks[2] * right_sig * (1.0 - right_sig),
            grad_logit,
        ],
        axis=0,
    ).astype(jnp.bfloat16)
    grad_in = jnp.einsum("ep,de->pd", grad_proj, proj_weight, preferred_element_type=jnp.float32)
    grad_pair = norm_back(grad_in * in_gain, normed, scale_inv, -1)
    return grad_pair.astype(jnp.bfloat16).reshape(rows_here, cols_here, width)


def solution(mesh):
    placed = (P("row", "ch", None), P("row", "ch", None), P(), P(), P(), P(), P(), P())
    return jax.shard_map(
        on_device, mesh=mesh, in_specs=placed, out_specs=P("row", "ch", None), check_vma=False
    )
```

profile of v0, /device:TPU:1, one launch (start us, length us, event | category | flops | bytes accessed | tf_op | source)
XLA Modules:
  0.0 299.7 jit_solution(16252508146671583930)
XLA Ops:
  14.6 12.4 %all_to_all.99 = bf16[8,2,8192]{2,1,0:T(2,128)(2,1)} all-to-all(bf16[8,2,8192]{2,1,0:T(2,128)(2,1)} %reshape.139), channel_id=1, replica_groups=mesh['row'=32,'ch'=8] {'ch'}, dimensions={0} | all-to-all | bytes 524288 | tf_op jit(solution)/shard_map/all_to_all | solution.py:35
  34.1 10.2 %all_to_all.100 = bf16[8,2,8192]{2,1,0:T(2,128)(2,1)} all-to-all(bf16[8,2,8192]{2,1,0:T(2,128)(2,1)} %reshape.137), channel_id=1, replica_groups=mesh['row'=32,'ch'=8] {'ch'}, dimensions={0} | all-to-all | bytes 524288 | tf_op jit(solution)/shard_map/all_to_all | solution.py:34
  48.9 86.5 %all-gather.3.cloned.1.call-done = bf16[16,512,512]{2,1,0:T(8,128)(2,1)} async-done(((bf16[16,16,512]{2,1,0:T(8,128)(2,1)}), bf16[16,512,512]{2,1,0:T(8,128)(2,1)}) %all-gather.3.cloned.1.call-update) | async-done | bytes 8388624 | tf_op jit(solution)/shard_map/all_gather | solution.py:40
  135.5 5.8 %convolution_convert_fusion.2 = bf16[16,16,512]{2,1,0:T(8,128)(2,1)S(1)} fusion(bf16[16,16,512]{2,1,0:T(8,128)(2,1)} %all_to_all.76, bf16[16,512,512]{2,1,0:T(8,128)(2,1)} %all-gather.3.cloned.1.call-done), kind=kOutput, calls=%fused_computation.11 | convolution fusion | flops 134348800 | bytes 8912896 | tf_op jit(solution)/shard_map/cik,cjk->cij/dot_general | solution.py:37
  141.2 2.8 copy.35
  144.1 3.4 %reshape.141 = bf16[8,2,8192]{2,1,0:T(2,128)(2,1)S(1)} reshape(bf16[512,16,16]{2,1,0:T(8,128)(2,1)} %bitcast.113) | data formatting | bytes 524288
  147.5 11.2 %all_to_all.101 = bf16[8,2,8192]{2,1,0:T(2,128)(2,1)S(1)} all-to-all(bf16[8,2,8192]{2,1,0:T(2,128)(2,1)S(1)} %reshape.141), channel_id=1, replica_groups=mesh['row'=32,'ch'=8] {'ch'}, dimensions={0} | all-to-all | bytes 524288 | tf_op jit(solution)/shard_map/all_to_all | solution.py:43
  158.7 2.4 reshape.142
  161.1 3.6 %copy.36 = f32[16,16,8,64]{3,1,0,2:T(8,128)} copy(bf16[16,16,8,64]{1,0,3,2:T(8,128)(2,1)} %bitcast.114) | data formatting | bytes 786432 | tf_op jit(solution)/shard_map/convert_element_type | solution.py:44
  173.6 2.4 fusion.18
  178.4 10.3 %all_to_all.102 = bf16[8,2,8192]{2,1,0:T(2,128)(2,1)} all-to-all(bf16[8,2,8192]{2,1,0:T(2,128)(2,1)} %reshape.143), channel_id=1, replica_groups=mesh['row'=32,'ch'=8] {'ch'}, dimensions={0} | all-to-all | bytes 524288 | tf_op jit(solution)/shard_map/all_to_all | solution.py:56
  192.6 4.6 %convolution_convert_fusion.1 = bf16[16,16,512]{2,1,0:T(8,128)(2,1)S(1)} fusion(bf16[16,16,512]{2,1,0:T(8,128)(2,1)S(1)} %all_to_all.85, bf16[16,512,512]{2,1,0:T(8,128)(2,1)} %all-gather.3.cloned.1.call-done), kind=kOutput, calls=%fused_computation.10 | convolution fusion | flops 134348800 | bytes 8912896 | tf_op jit(solution)/shard_map/cij,cjk->cik/dot_general | solution.py:59
  197.2 2.8 copy.40
  200.0 4.0 %reshape.145 = bf16[8,2,8192]{2,1,0:T(2,128)(2,1)} reshape(bf16[512,16,16]{2,1,0:T(8,128)(2,1)} %bitcast.115) | data formatting | bytes 524288
  204.0 3.4 %all-to-all-start.4 = ((bf16[8,2,8192]{2,1,0:T(2,128)(2,1)}), bf16[8,2,8192]{2,1,0:T(2,128)(2,1)S(1)}, u32[]{:S(2)}, u32[]{:S(2)}) async-start(bf16[8,2,8192]{2,1,0:T(2,128)(2,1)} %reshape.145), calls=%async_computation.4 | async-start | bytes 524288 | tf_op jit(solution)/shard_map/all_to_all | solution.py:73
  207.4 2.8 copy.44
  210.2 4.4 %reshape.147 = bf16[32,2,2048]{2,1,0:T(2,128)(2,1)} reshape(bf16[512,16,16]{2,1,0:T(8,128)(2,1)} %bitcast.116) | data formatting | bytes 524288
  214.6 7.8 %all-to-all-start.5 = ((bf16[32,2,2048]{2,1,0:T(2,128)(2,1)}), bf16[32,2,2048]{2,1,0:T(2,128)(2,1)}, u32[]{:S(2)}, u32[]{:S(2)}) async-start(bf16[32,2,2048]{2,1,0:T(2,128)(2,1)} %reshape.147), calls=%async_computation.5 | async-start | bytes 524288 | tf_op jit(solution)/shard_map/all_to_all | solution.py:57
  222.4 2.4 reshape.146
  224.8 3.6 %copy.41 = f32[16,16,8,64]{3,1,0,2:T(8,128)} copy(bf16[16,16,8,64]{1,0,3,2:T(8,128)(2,1)} %bitcast.117) | data formatting | bytes 786432 | tf_op jit(solution)/shard_map/convert_element_type | solution.py:80
  228.4 2.4 reshape.130
  233.0 5.5 %all-to-all-done.5 = bf16[32,2,2048]{2,1,0:T(2,128)(2,1)} async-done(((bf16[32,2,2048]{2,1,0:T(2,128)(2,1)}), bf16[32,2,2048]{2,1,0:T(2,128)(2,1)}, u32[]{:S(2)}, u32[]{:S(2)}) %all-to-all-start.5) | async-done | bytes 262176 | tf_op jit(solution)/shard_map/all_to_all | solution.py:57
  238.5 3.6 %reshape.148 = bf16[512,16,16]{2,1,0:T(8,128)(2,1)} reshape(bf16[32,2,2048]{2,1,0:T(2,128)(2,1)} %all-to-all-done.5) | data formatting | bytes 524288
  242.1 4.2 %copy.46 = bf16[16,32,16,16]{2,1,3,0:T(8,128)(2,1)} copy(bf16[16,32,16,16]{2,0,3,1:T(8,128)(2,1)} %bitcast.120) | data formatting | bytes 524288 | tf_op jit(solution)/shard_map/all_to_all | solution.py:57
  246.4 5.1 %all_to_all.90 = bf16[16,512,16]{1,2,0:T(8,128)(2,1)} reshape(bf16[16,32,16,16]{2,1,3,0:T(8,128)(2,1)} %copy.46) | data formatting | bytes 524288 | tf_op jit(solution)/shard_map/all_to_all | solution.py:57
  251.5 5.4 %convolution_convert_fusion = bf16[16,16,512]{2,1,0:T(8,128)(2,1)} fusion(bf16[16,512,16]{1,2,0:T(8,128)(2,1)} %all_to_all.90, bf16[16,512,512]{2,1,0:T(8,128)(2,1)} %all-gather.5.cloned.1.call-done), kind=kOutput, calls=%fused_computation.9 | convolution fusion | flops 134348800 | bytes 8912896 | tf_op jit(solution)/shard_map/cij,cik->cjk/dot_general | solution.py:66
  256.9 3.7 %copy.47 = bf16[16,16,512]{1,0,2:T(8,128)(2,1)} copy(bf16[16,16,512]{2,1,0:T(8,128)(2,1)} %convolution_convert_fusion) | data formatting | bytes 524288 | tf_op jit(solution)/shard_map/convert_element_type | solution.py:77
  260.6 4.0 %reshape.149 = bf16[8,2,8192]{2,1,0:T(2,128)(2,1)} reshape(bf16[512,16,16]{2,1,0:T(8,128)(2,1)} %bitcast.118) | data formatting | bytes 524288
  264.6 4.7 %all-to-all-start.6 = ((bf16[8,2,8192]{2,1,0:T(2,128)(2,1)}), bf16[8,2,8192]{2,1,0:T(2,128)(2,1)}, u32[]{:S(2)}, u32[]{:S(2)}) async-start(bf16[8,2,8192]{2,1,0:T(2,128)(2,1)} %reshape.149), calls=%async_computation.6 | async-start | bytes 524288 | tf_op jit(solution)/shard_map/all_to_all | solution.py:76
  270.3 5.7 %all-to-all-done.6 = bf16[8,2,8192]{2,1,0:T(2,128)(2,1)} async-done(((bf16[8,2,8192]{2,1,0:T(2,128)(2,1)}), bf16[8,2,8192]{2,1,0:T(2,128)(2,1)}, u32[]{:S(2)}, u32[]{:S(2)}) %all-to-all-start.6) | async-done | bytes 262176 | tf_op jit(solution)/shard_map/all_to_all | solution.py:76
  275.9 3.4 %reshape.150 = bf16[512,16,16]{2,1,0:T(8,128)(2,1)} reshape(bf16[8,2,8192]{2,1,0:T(2,128)(2,1)} %all-to-all-done.6) | data formatting | bytes 524288
  279.3 3.6 %copy.48 = f32[16,16,8,64]{3,1,0,2:T(8,128)} copy(bf16[16,16,8,64]{1,0,3,2:T(8,128)(2,1)} %bitcast.119) | data formatting | bytes 786432 | tf_op jit(solution)/shard_map/convert_element_type | solution.py:81
  (71 shorter events, 47.7 us)
Async XLA Ops:
  6.5 4.0 %copy-start = (bf16[128,640]{1,0:T(8,128)(2,1)S(1)}, bf16[128,640]{1,0:T(8,128)(2,1)}, u32[]{:S(2)}) copy-start(bf16[128,640]{1,0:T(8,128)(2,1)} %param.12) | copy-start | bytes 491524
  6.5 128.9 %all-gather.3.cloned.1.call-start = ((), (), s32[]{:S(2)}) async-start(), calls=%async_computation.7 | async-start | bytes 8650752 | tf_op jit(solution)/shard_map/all_gather | solution.py:40
  31.6 219.9 %all-gather.5.cloned.1.call-start = ((), (), s32[]{:S(2)}) async-start(), calls=%async_computation.8 | async-start | bytes 8650752 | tf_op jit(solution)/shard_map/all_gather | solution.py:69
  164.7 5.6 %copy-start.6 = (bf16[128,128]{1,0:T(8,128)(2,1)S(1)}, bf16[128,128]{1,0:T(8,128)(2,1)}, u32[]{:S(2)}) copy-start(bf16[128,128]{1,0:T(8,128)(2,1)} %param.15) | copy-start | bytes 98308
  164.7 5.6 %copy-start.7 = (f32[128]{0:T(128)S(1)}, f32[128]{0:T(128)}, u32[]{:S(2)}) copy-start(f32[128]{0:T(128)} %param.13) | copy-start | bytes 1540
  167.3 3.0 %copy-start.2 = (f32[128,1024]{0,1:T(8,128)S(1)}, f32[128,1024]{0,1:T(8,128)}, u32[]{:S(2)}) copy-start(f32[128,1024]{0,1:T(8,128)} %copy.37) | copy-start | bytes 1572868
  204.0 10.6 %all-to-all-start.4 = ((bf16[8,2,8192]{2,1,0:T(2,128)(2,1)}), bf16[8,2,8192]{2,1,0:T(2,128)(2,1)S(1)}, u32[]{:S(2)}, u32[]{:S(2)}) async-start(bf16[8,2,8192]{2,1,0:T(2,128)(2,1)} %reshape.145), calls=%async_computation.4 | async-start | bytes 524288 | tf_op jit(solution)/shard_map/all_to_all | solution.py:73
  214.6 23.9 %all-to-all-start.5 = ((bf16[32,2,2048]{2,1,0:T(2,128)(2,1)}), bf16[32,2,2048]{2,1,0:T(2,128)(2,1)}, u32[]{:S(2)}, u32[]{:S(2)}) async-start(bf16[32,2,2048]{2,1,0:T(2,128)(2,1)} %reshape.147), calls=%async_computation.5 | async-start | bytes 524288 | tf_op jit(solution)/shard_map/all_to_all | solution.py:57
  264.6 11.3 %all-to-all-start.6 = ((bf16[8,2,8192]{2,1,0:T(2,128)(2,1)}), bf16[8,2,8192]{2,1,0:T(2,128)(2,1)}, u32[]{:S(2)}, u32[]{:S(2)}) async-start(bf16[8,2,8192]{2,1,0:T(2,128)(2,1)} %reshape.149), calls=%async_computation.6 | async-start | bytes 524288 | tf_op jit(solution)/shard_map/all_to_all | solution.py:76
  285.2 3.0 %copy-start.8 = (f32[128]{0:T(128)S(1)}, f32[128]{0:T(128)}, u32[]{:S(2)}) copy-start(f32[128]{0:T(128)} %param.14) | copy-start | bytes 1540
  286.5 1.8 copy-start.3
  286.5 1.8 copy-start.5
  288.3 1.2 copy-start.1
  288.3 1.2 copy-start.4
Sparse Core Ops, SparseCore 0:
  31.7 103.7 all-gather.2
  138.3 107.7 all-gather.4
where the time goes:
time: 302 us; the launch traced here: 300 us
  waiting for transfers between devices  97.8 us (32%)
  local copies, waits for them, and re-layouts  90.4 us (30%)
  blocking collectives  44.2 us (15%)
  matrix products  21.5 us (7%)
  other arithmetic  16.3 us (5%)
  starting transfers between devices  16 us (5%)
  between operations  13.6 us (5%)
    all_gather x1, waiting for transfers between devices, on_device(): lax.all_gather(right_chan, 'row', axis=1, tiled=True)  86.5 us
    unnamed x32, local copies, waits for them, and re-layouts  35 us
    all_to_all x1, blocking collectives, on_device(): lax.all_to_all(right_fac, 'ch', split_axis=0, concat_axis=2, tiled=True)  12.4 us
    all_to_all x1, blocking collectives, on_device(): lax.all_to_all(tri_chan, 'ch', split_axis=2, concat_axis=0, tiled=True)  11.2 us
    all_to_all x1, blocking collectives, on_device(): lax.all_to_all(grad_tri, 'ch', split_axis=0, concat_axis=2, tiled=True)  10.3 us
    all_to_all x1, blocking collectives, on_device(): lax.all_to_all(left_fac, 'ch', split_axis=0, concat_axis=2, tiled=True)  10.2 us
    all_to_all x2, local copies, waits for them, and re-layouts, on_device(): lax.all_to_all(grad_chan, 'row', split_axis=2, concat_axis=1, tiled=True)  9.37 us
    all_to_all x1, starting transfers between devices, on_device(): lax.all_to_all(grad_chan, 'row', split_axis=2, concat_axis=1, tiled=True)  7.83 us
  transfers between devices with their start and end apart: 5, of which 3 were waited for; matrix products, arithmetic and copies ran while one was open for 26% of the time, Pallas kernels for 0%

commit v1 on v0

v1 whole, which is shorter than its diff:
```python
import functools

import jax
import jax.numpy as jnp
from jax import lax
from jax.experimental import pallas as pl
from jax.experimental.pallas import tpu as pltpu
from jax.sharding import PartitionSpec as P

EPSILON = 1e-05
MESH = pl.DeviceIdType.MESH
F32 = jnp.float32
BF16 = jnp.bfloat16
C = 128
N = 512
CHIPS = 128
GROUPS = 8
STRIDE = 37


def nt(a, b):
    return lax.dot_general(a, b, (((1,), (1,)), ((), ())), preferred_element_type=F32)


def nn(a, b):
    return lax.dot_general(a, b, (((1,), (0,)), ((), ())), preferred_element_type=F32)


def swap_halves(a, b):
    axis = a.ndim - 1
    low = lax.broadcasted_iota(jnp.int32, a.shape, axis) < 64
    return (
        jnp.where(low, a, pltpu.roll(b, 64, axis)),
        jnp.where(low, pltpu.roll(a, 64, axis), b),
    )


def column(row_ref):
    return jnp.broadcast_to(row_ref[...], (C, C)).T


def body(
    x_ref, cot_ref, ig_ref, ib_ref, w_ref, og_ref, ob_ref, ow_ref, out_ref,
    wt, owt,
    normed, sinv, left_a, left_b, right_a, right_b, gate, cot_t, grad_acc,
    hid, stage, stage2,
    r_send, r_all, l_send, l_all, t_send, t_recv, g_send, g_all,
    gl_send, gl_recv, gr_send, gr_recv,
    r_f32, r_mat, l_mat, gt_mat, gtt, gr_f32,
    send_sem, recv_sem, core_send, core_recv,
):
    row = lax.axis_index("row")
    ch = lax.axis_index("ch")
    core = lax.rem(row, 2)
    other = 1 - core
    me = (row // 2) * 8 + ch
    partner = (row + 1 - 2 * core, ch)

    def device(chip):
        return ((chip // 8) * 2 + core, lax.rem(chip, 8))

    barrier = pltpu.get_barrier_semaphore()

    def greet(step, carry):
        pl.semaphore_signal(
            barrier, inc=1, device_id=device(lax.rem(me + step, CHIPS)), device_id_type=MESH
        )
        return carry

    pl.semaphore_signal(barrier, inc=1, device_id=partner, device_id_type=MESH)
    lax.fori_loop(1, CHIPS, greet, 0)

    def exchange(which, source, target):
        own = pltpu.make_async_copy(source.at[me], target.at[me], recv_sem.at[which])
        own.start()

        def send(step, carry):
            chip = lax.rem(me + lax.rem(step * STRIDE, CHIPS), CHIPS)
            pltpu.make_async_remote_copy(
                src_ref=source.at[chip],
                dst_ref=target.at[me],
                send_sem=send_sem.at[which],
                recv_sem=recv_sem.at[which],
                device_id=device(chip),
                device_id_type=MESH,
            ).start()
            return carry

        lax.fori_loop(1, CHIPS, send, 0)

    def arrived(which, target):
        pltpu.make_async_copy(target, target, recv_sem.at[which]).wait()

    def sent(which, source):
        most = source.at[pl.ds(0, CHIPS - 1)]
        pltpu.make_async_copy(most, most, send_sem.at[which]).wait()

    def to_partner(which, buffer):
        copy = pltpu.make_async_remote_copy(
            src_ref=buffer.at[core],
            dst_ref=buffer.at[core],
            send_sem=core_send.at[which],
            recv_sem=core_recv.at[which],
            device_id=partner,
            device_id_type=MESH,
        )
        copy.start()

    def from_partner(which, buffer):
        pltpu.make_async_copy(buffer.at[other], buffer.at[other], core_recv.at[which]).wait()

    def to_partner_sent(which, buffer):
        pltpu.make_async_copy(buffer.at[core], buffer.at[core], core_send.at[which]).wait()

    wt[...] = w_ref[...].astype(F32).T.astype(BF16)
    in_gain = column(ig_ref)
    in_bias = column(ib_ref)
    normals = []
    for g in range(GROUPS):
        x = x_ref[pl.ds(g * 128, 128), :].astype(F32).T
        shifted = x - jnp.sum(x, axis=0, keepdims=True) * (1.0 / C)
        scale = lax.rsqrt(jnp.sum(shifted * shifted, axis=0, keepdims=True) * (1.0 / C) + EPSILON)
        hat = shifted * scale
        normed[g] = hat
        sinv[g] = jnp.broadcast_to(scale, (8, 128))
        normal = (hat * in_gain + in_bias).astype(BF16)
        normals.append(normal)
        projected = nn(wt[pl.ds(256, 256), :], normal)
        val, sig = projected[:128], jax.nn.sigmoid(projected[128:])
        factor = sig * val
        right_a[g] = sig
        right_b[g] = factor * (1.0 - sig)
        stage[pl.ds(g, C, stride=8), :] = factor
    r_send[...] = stage[...].reshape(C, 8, 128).astype(BF16)
    pl.semaphore_wait(barrier, CHIPS)
    exchange(0, r_send, r_all.at[core])

    for g in range(GROUPS):
        projected = nn(wt[pl.ds(0, 256), :], normals[g])
        val, sig = projected[:128], jax.nn.sigmoid(projected[128:])
        factor = sig * val
        left_a[g] = sig
        left_b[g] = factor * (1.0 - sig)
        stage2[pl.ds(g, C, stride=8), :] = factor
    l_send[...] = stage2[...].reshape(C, 8, 128).astype(BF16)
    exchange(1, l_send, l_all.at[core])

    owt[...] = ow_ref[...].astype(F32).T.astype(BF16)
    out_gain = column(og_ref)
    mean_h = []
    for g in range(GROUPS):
        out_gate = jax.nn.sigmoid(nn(wt[pl.ds(512, 128), :], normals[g]))
        cotangent = cot_ref[pl.ds(g * 128, 128), :].astype(F32).T
        grad_mixed = cotangent * out_gate
        gate[g] = out_gate
        cot_t[g] = cotangent
        h = nn(ow_ref[...], grad_mixed.astype(BF16)) * out_gain
        hid[pl.ds(g, C, stride=8), :] = h
        mean_h.append(jnp.sum(h, axis=0, keepdims=True) * (1.0 / C))
    mean_h = jnp.concatenate(mean_h, axis=0)

    def place_right(slot):
        tiles = r_all[slot].reshape(16, 8, 8, 128)
        for pair in range(4):
            a = tiles[:, 2 * pair].astype(F32)
            b = tiles[:, 2 * pair + 1].astype(F32)
            even, odd = swap_halves(a, b)
            r_f32[pair, :, pl.ds(16 * slot, 8, stride=2), :] = even
            r_f32[pair, :, pl.ds(16 * slot + 1, 8, stride=2), :] = odd

    def place_pairs(buffer, slot, matrix):
        tiles = buffer[slot].reshape(16, 8, 8, 128)
        for pair in range(4):
            a = tiles[:, 2 * pair].astype(F32).reshape(128, 128)
            b = tiles[:, 2 * pair + 1].astype(F32).reshape(128, 128)
            even, odd = swap_halves(a, b)
            lanes = pl.ds(128 * pair, 128)
            matrix[slot, 0, :, lanes] = even.astype(BF16)
            matrix[slot, 1, :, lanes] = odd.astype(BF16)

    def quarter(matrix, pair):
        return matrix[:, 128 * pair : 128 * pair + 128]

    def pieces(even, odd, buffer):
        for pair in range(4):
            a, b = swap_halves(even(pair), odd(pair))
            a = a.reshape(16, 8, 128).astype(BF16)
            b = b.reshape(16, 8, 128).astype(BF16)
            for q in range(16):
                buffer[8 * q + 2 * pair] = a[q]
                buffer[8 * q + 2 * pair + 1] = b[q]

    arrived(0, r_all.at[core])
    to_partner(0, r_all)
    from_partner(0, r_all)
    place_right(0)
    place_right(1)
    for pair in range(4):
        r_mat[:, pl.ds(128 * pair, 128)] = r_f32[pair].reshape(N, 128).astype(BF16)

    arrived(1, l_all.at[core])
    to_partner(1, l_all)
    place_pairs(l_all, core, l_mat)
    tri = [nt(l_mat[core, parity], r_mat[...]) for parity in range(2)]
    pieces(functools.partial(quarter, tri[0]), functools.partial(quarter, tri[1]), t_send)
    exchange(2, t_send, t_recv)
    from_partner(1, l_all)
    place_pairs(l_all, other, l_mat)

    arrived(2, t_recv)
    tri = t_recv[...].astype(F32)
    mean_tri = jnp.sum(tri, axis=0) * (1.0 / C)
    shifted = tri - mean_tri[None]
    scale_tri = lax.rsqrt(jnp.sum(shifted * shifted, axis=0) * (1.0 / C) + EPSILON)
    h = hid[...].reshape(C, 8, 128)
    second = jnp.sum(h * shifted, axis=0) * (scale_tri * (1.0 / C))
    grad_tri = scale_tri[None] * (h - mean_h[None] - shifted * (scale_tri * second)[None])
    g_send[...] = grad_tri.astype(BF16)
    exchange(3, g_send, g_all.at[core])

    stage[...] = (shifted * scale_tri[None]).reshape(C * 8, 128)
    out_bias = column(ob_ref)
    for g in range(GROUPS):
        hat = stage[pl.ds(g, C, stride=8), :]
        mixed = nn(owt[...], (hat * out_gain + out_bias).astype(BF16))
        out_gate = gate[g]
        grad_logit = cot_t[g] * mixed * out_gate * (1.0 - out_gate)
        grad_acc[g] = nn(w_ref[:, pl.ds(512, 128)], grad_logit.astype(BF16))

    arrived(3, g_all.at[core])
    to_partner(2, g_all)
    place_pairs(g_all, core, gt_mat)
    grad = [nn(gt_mat[core, parity], r_mat[...]) for parity in range(2)]
    pieces(functools.partial(quarter, grad[0]), functools.partial(quarter, grad[1]), gl_send)
    exchange(4, gl_send, gl_recv)
    from_partner(2, g_all)
    place_pairs(g_all, other, gt_mat)
    total = None
    for slot in range(2):
        for parity in range(2):
            gtt[...] = gt_mat[slot, parity].astype(F32).T.reshape(16, 32, 128)
            mine = gtt[:, pl.ds(16 * core, 16), :].reshape(256, 128).astype(BF16)
            part = nn(mine, l_mat[slot, parity])
            total = part if total is None else total + part
    for pair in range(4):
        gr_f32[pair] = quarter(total, pair).reshape(16, 16, 128)
    pieces(
        lambda pair: gr_f32[pair, :, pl.ds(0, 8, stride=2), :].reshape(128, 128),
        lambda pair: gr_f32[pair, :, pl.ds(1, 8, stride=2), :].reshape(128, 128),
        gr_send,
    )
    exchange(5, gr_send, gr_recv)

    arrived(4, gl_recv)
    stage2[...] = gl_recv[...].astype(F32).reshape(C * 8, 128)
    for g in range(GROUPS):
        grad = stage2[pl.ds(g, C, stride=8), :]
        both = jnp.concatenate([grad * left_a[g], grad * left_b[g]], axis=0).astype(BF16)
        grad_acc[g] += nn(w_ref[:, pl.ds(0, 256)], both)

    arrived(5, gr_recv)
    stage[...] = gr_recv[...].astype(F32).reshape(C * 8, 128)
    for g in range(GROUPS):
        grad = stage[pl.ds(g, C, stride=8), :]
        both = jnp.concatenate([grad * right_a[g], grad * right_b[g]], axis=0).astype(BF16)
        full = (grad_acc[g] + nn(w_ref[:, pl.ds(256, 256)], both)) * in_gain
        hat = normed[g]
        first = jnp.sum(full, axis=0, keepdims=True) * (1.0 / C)
        second = jnp.sum(full * hat, axis=0, keepdims=True) * (1.0 / C)
        grad_pair = sinv[g][:1] * (full - first - hat * second)
        out_ref[pl.ds(g * 128, 128), :] = grad_pair.T.astype(BF16)

    for which, source in enumerate((r_send, l_send, t_send, g_send, gl_send, gr_send)):
        sent(which, source)
    for which, buffer in enumerate((r_all, l_all, g_all)):
        to_partner_sent(which, buffer)


def on_device(pair_act, cotangent, in_gain, in_bias, proj_weight, out_gain, out_bias, out_weight):
    pairs = pair_act.shape[0] * pair_act.shape[1]
    tiles = pltpu.VMEM((C, 8, 128), BF16)
    both = pltpu.VMEM((2, C, 8, 128), BF16)
    kept = pltpu.VMEM((GROUPS, C, 128), F32)
    flat = pltpu.VMEM((C * 8, 128), F32)
    out = pl.pallas_call(
        body,
        out_shape=jax.ShapeDtypeStruct((pairs, C), BF16),
        in_specs=[pl.BlockSpec(memory_space=pltpu.VMEM)] * 8,
        out_specs=pl.BlockSpec(memory_space=pltpu.VMEM),
        scratch_shapes=[
            pltpu.VMEM((5 * C, C), BF16),
            pltpu.VMEM((C, C), BF16),
            kept,
            pltpu.VMEM((GROUPS, 8, 128), F32),
            kept, kept, kept, kept, kept, kept, kept,
            flat, flat, flat,
            tiles, both, tiles, both, tiles, tiles, tiles, both,
            tiles, tiles, tiles, tiles,
            pltpu.VMEM((4, 16, 32, 128), F32),
            pltpu.VMEM((N, N), BF16),
            pltpu.VMEM((2, 2, 128, N), BF16),
            pltpu.VMEM((2, 2, 128, N), BF16),
            pltpu.VMEM((16, 32, 128), F32),
            pltpu.VMEM((4, 16, 16, 128), F32),
            pltpu.SemaphoreType.DMA((6,)),
            pltpu.SemaphoreType.DMA((6,)),
            pltpu.SemaphoreType.DMA((3,)),
            pltpu.SemaphoreType.DMA((3,)),
        ],
        compiler_params=pltpu.CompilerParams(
            collective_id=0, has_side_effects=True, vmem_limit_bytes=48 << 20
        ),
    )(
        pair_act.reshape(pairs, C),
        cotangent.reshape(pairs, C),
        in_gain.reshape(1, C),
        in_bias.reshape(1, C),
        proj_weight,
        out_gain.reshape(1, C),
        out_bias.reshape(1, C),
        out_weight,
    )
    return out.reshape(pair_act.shape)


def solution(mesh):
    placed = (P("row", "ch", None), P("row", "ch", None), P(), P(), P(), P(), P(), P())
    return jax.shard_map(
        on_device, mesh=mesh, in_specs=placed, out_specs=P("row", "ch", None), check_vma=False
    )
```

time: 302 us -> 70.6 us (0.23)
  waiting for transfers between devices: 97.8 us -> 0 us
  local copies, waits for them, and re-layouts: 90.4 us -> 4.97 us
  Pallas kernels: 0 us -> 65.3 us
  blocking collectives: 44.2 us -> 0 us
  matrix products: 21.5 us -> 0 us
  other arithmetic: 16.3 us -> 0 us
  starting transfers between devices: 16 us -> 0 us
  between operations: 13.6 us -> 0.03 us
    all_gather x2 -> x0, waiting for transfers between devices: 86.5 us -> none  [the longest x1 86.5 us: on_device(): lax.all_gather(right_chan, 'row', axis=1, tiled=True)]
    pallas_call x0 -> x1, Pallas kernels: none -> 65.3 us  [on_device(): pl.pallas_call(body, out_shape=jax.ShapeDtypeStruct((pairs, C), BF16), in...]
    all_to_all x4 -> x0, blocking collectives: 44.2 us -> none  [the longest x1 12.4 us: on_device(): lax.all_to_all(right_fac, 'ch', split_axis=0, concat_axis=2, tiled=True)]
    unnamed x32 -> x17, local copies, waits for them, and re-layouts: 35 us -> 4.97 us
    convert_element_type x12 -> x0, local copies, waits for them, and re-layouts: 29.9 us -> none  [the longest x3 7.24 us: on_device(): left_grad = left_back.astype(jnp.float32).reshape(width, -1)]
    dot_general x7 -> x0, matrix products: 21.5 us -> none  [the longest x1 5.76 us: on_device(): jnp.einsum('cik,cjk->cij', left_chan, lax.all_gather(right_chan, 'row', a...]
    all_to_all x9 -> x0, local copies, waits for them, and re-layouts: 21.1 us -> none  [the longest x2 9.37 us: on_device(): lax.all_to_all(grad_chan, 'row', split_axis=2, concat_axis=1, tiled=True)]
    all_to_all x3 -> x0, starting transfers between devices: 16 us -> none  [the longest x1 7.83 us: on_device(): lax.all_to_all(grad_chan, 'row', split_axis=2, concat_axis=1, tiled=True)]
  transfers between devices with their start and end apart: 5 -> 0, of which waited for: 3 -> 0; matrix products, arithmetic and copies ran while one was open for 26% -> 0% of each run, Pallas kernels for 0% -> 0%
where the time goes in v1:
time: 70.6 us; the launch traced here: 70.3 us
  Pallas kernels  65.3 us (92%)
  local copies, waits for them, and re-layouts  4.97 us (7%)
    pallas_call x1, Pallas kernels, on_device(): pl.pallas_call(body, out_shape=jax.ShapeDtypeStruct((pairs, C), BF16), in...  65.3 us
    unnamed x17, local copies, waits for them, and re-layouts  4.97 us

profile of v1, /device:TPU:1, one launch (start us, length us, event | category | flops | bytes accessed | tf_op | source)
XLA Modules:
  0.0 70.3 jit_solution(9666162989833319549)
XLA Ops:
  0.0 0.0 copy-start.7
  0.0 0.0 copy-start.4
  0.0 0.0 copy-start.5
  0.0 0.0 copy-start.6
  0.0 0.6 copy-done.7
  0.7 0.0 copy-done.4
  0.7 0.0 copy-done.5
  0.7 0.0 copy-done.6
  0.7 0.0 copy-start
  0.7 0.9 %copy-done = bf16[16,64,128]{2,1,0:T(8,128)(2,1)S(1)} copy-done((bf16[16,64,128]{2,1,0:T(8,128)(2,1)S(1)}, bf16[16,64,128]{2,1,0:T(8,128)(2,1)}, u32[]{:S(2)}) %copy-start) | copy-done | bytes 262168
  1.7 0.0 copy-start.1
  1.7 0.9 %copy-done.1 = bf16[16,64,128]{2,1,0:T(8,128)(2,1)S(1)} copy-done((bf16[16,64,128]{2,1,0:T(8,128)(2,1)S(1)}, bf16[16,64,128]{2,1,0:T(8,128)(2,1)}, u32[]{:S(2)}) %copy-start.1) | copy-done | bytes 262168
  2.6 0.0 copy-start.2
  2.6 0.9 %copy-done.2 = bf16[128,640]{1,0:T(8,128)(2,1)S(1)} copy-done((bf16[128,640]{1,0:T(8,128)(2,1)S(1)}, bf16[128,640]{1,0:T(8,128)(2,1)}, u32[]{:S(2)}) %copy-start.2) | copy-done | bytes 163864
  3.5 0.0 copy-start.3
  3.5 0.8 %copy-done.3 = bf16[128,128]{1,0:T(8,128)(2,1)S(1)} copy-done((bf16[128,128]{1,0:T(8,128)(2,1)S(1)}, bf16[128,128]{1,0:T(8,128)(2,1)}, u32[]{:S(2)}) %copy-start.3) | copy-done | bytes 32792
  4.3 65.3 %shard_map.82 = bf16[1024,128]{1,0:T(8,128)(2,1)S(1)} custom-call(bf16[1024,128]{1,0:T(8,128)(2,1)S(1)} %bitcast.8, bf16[1024,128]{1,0:T(8,128)(2,1)S(1)} %bitcast.9, f32[1,128]{1,0:T(1,128)S(1)} %bitcast.10, f32[1,128]{1,0:T(1,128)S(1)} %bitcast.11, bf16[128,640]{1,0:T(8,128)(2,1)S(1)} %copy-done.2, f32[1,128]{1,0:T(1,128)S(1)} %bitcast.12, ...), custom_call_target="tpu_custom_call" | custom-call | tf_op jit(solution)/shard_map/pallas_call | solution.py:285
  69.6 0.7 %copy.10 = bf16[16,64,128]{2,1,0:T(8,128)(2,1)} copy(bf16[16,64,128]{2,1,0:T(8,128)(2,1)S(1)} %bitcast.7) | data formatting | bytes 524288
Async XLA Ops:
  0.0 0.7 copy-start.7
  0.0 0.7 copy-start.4
  0.0 0.7 copy-start.5
  0.0 0.7 copy-start.6
  0.7 0.9 %copy-start = (bf16[16,64,128]{2,1,0:T(8,128)(2,1)S(1)}, bf16[16,64,128]{2,1,0:T(8,128)(2,1)}, u32[]{:S(2)}) copy-start(bf16[16,64,128]{2,1,0:T(8,128)(2,1)} %param.8) | copy-start | bytes 786436
  1.7 0.9 %copy-start.1 = (bf16[16,64,128]{2,1,0:T(8,128)(2,1)S(1)}, bf16[16,64,128]{2,1,0:T(8,128)(2,1)}, u32[]{:S(2)}) copy-start(bf16[16,64,128]{2,1,0:T(8,128)(2,1)} %param.9) | copy-start | bytes 786436
  2.6 0.9 %copy-start.2 = (bf16[128,640]{1,0:T(8,128)(2,1)S(1)}, bf16[128,640]{1,0:T(8,128)(2,1)}, u32[]{:S(2)}) copy-start(bf16[128,640]{1,0:T(8,128)(2,1)} %w_ref.1) | copy-start | bytes 491524
  3.5 0.8 %copy-start.3 = (bf16[128,128]{1,0:T(8,128)(2,1)S(1)}, bf16[128,128]{1,0:T(8,128)(2,1)}, u32[]{:S(2)}) copy-start(bf16[128,128]{1,0:T(8,128)(2,1)} %ow_ref.1) | copy-start | bytes 98308

commit v2 on v1

v2 whole, which is shorter than its diff:
```python
import jax
import jax.numpy as jnp
from jax import lax
from jax.experimental import pallas as pl
from jax.experimental.pallas import tpu as pltpu
from jax.sharding import PartitionSpec as P

EPSILON = 1e-05
MESH = pl.DeviceIdType.MESH
F32 = jnp.float32
BF16 = jnp.bfloat16
C = 128
N = 512
GROUPS = 8
PLANES = 8
FAR = (2, 1, 3, 0)
RIGHT, LEFT, TRI, GRAD, GRAD_LEFT, GRAD_RIGHT = range(6)


def nn(a, b):
    return lax.dot_general(a, b, (((1,), (0,)), ((), ())), preferred_element_type=F32)


def swap_halves(a, b):
    axis = a.ndim - 1
    low = lax.broadcasted_iota(jnp.int32, a.shape, axis) < 64
    return (
        jnp.where(low, a, pltpu.roll(b, 64, axis)),
        jnp.where(low, pltpu.roll(a, 64, axis), b),
    )


def column(row_ref):
    return jnp.broadcast_to(row_ref[...], (C, C)).T


def distance(n):
    return 4 + ((n + 1) // 2) * (1 - 2 * lax.rem(n, 2))


def body(
    x_hbm, cot_hbm, ig_hbm, ib_hbm, w_hbm, og_hbm, ob_hbm, ow_hbm, out_ref,
    x_ref, cot_ref, ig_ref, ib_ref, w_ref, og_ref, ob_ref, ow_ref,
    wt, owt,
    normal, normed, sinv, left_a, left_b, right_a, right_b, gate, cot_t, grad_acc,
    hid, shift, stage,
    r_send, r_all, l_send, l_all, t_send, t_recv, g_send, g_all,
    gl_send, gl_recv, gr_send, gr_recv,
    r_f32, r_mat, r_matt, l_mat, gt_mat, gtt, gr_f32,
    in_sem, send_sem, recv_sem, core_send, core_recv,
):
    row = lax.axis_index("row")
    ch = lax.axis_index("ch")
    core = lax.rem(row, 2)
    other = 1 - core
    z = lax.rem(row // 2, 8)
    y = (row // 16) * 2 + ch // 4
    x = lax.rem(ch, 4)
    me = z * 16 + (row // 16) * 8 + ch
    partner = (row + 1 - 2 * core, ch)

    loads = [
        pltpu.make_async_copy(source, target, in_sem.at[i])
        for i, (source, target) in enumerate((
            (x_hbm, x_ref), (w_hbm, w_ref), (ig_hbm, ig_ref), (ib_hbm, ib_ref),
            (cot_hbm, cot_ref), (og_hbm, og_ref), (ob_hbm, ob_ref), (ow_hbm, ow_ref),
        ))
    ]
    for load in loads:
        load.start()

    ys = [lax.rem(y + d, 4) for d in FAR]
    xs = [lax.rem(x + d, 4) for d in FAR]
    chips = [(yy // 2, lax.rem(yy, 2) * 4 + xx) for yy in ys for xx in xs]

    def device(plane, chip):
        return ((chip[0] * 8 + plane) * 2 + core, chip[1])

    def slot(plane, chip):
        return plane * 16 + chip[0] * 8 + chip[1]

    def each_plane(step):
        lax.fori_loop(0, PLANES, lambda n, carry: (step(n), carry)[1], 0)

    barrier = pltpu.get_barrier_semaphore()
    pl.semaphore_signal(barrier, inc=1, device_id=partner, device_id_type=MESH)

    def greet(n):
        plane = lax.rem(z + distance(n), PLANES)
        for chip in chips[:-1]:
            pl.semaphore_signal(
                barrier, inc=1, device_id=device(plane, chip), device_id_type=MESH
            )

        @pl.when(n < PLANES - 1)
        def _():
            pl.semaphore_signal(
                barrier, inc=1, device_id=device(plane, chips[-1]), device_id_type=MESH
            )

    each_plane(greet)

    def send_plane(which, n, source, target):
        plane = lax.rem(z + distance(n), PLANES)

        def send(chip):
            pltpu.make_async_remote_copy(
                src_ref=source.at[slot(plane, chip)],
                dst_ref=target.at[me],
                send_sem=send_sem.at[which],
                recv_sem=recv_sem.at[which, z],
                device_id=device(plane, chip),
                device_id_type=MESH,
            ).start()

        for chip in chips[:-1]:
            send(chip)

        @pl.when(n < PLANES - 1)
        def _():
            send(chips[-1])

        @pl.when(n == PLANES - 1)
        def _():
            pltpu.make_async_copy(source.at[me], target.at[me], recv_sem.at[which, z]).start()

    def going_to(n):
        return lax.rem(z + distance(n), PLANES)

    def coming_from(n):
        return lax.rem(z + PLANES - distance(n), PLANES)

    def tiles(plane):
        return pl.ds(pl.multiple_of(plane * 16, 16), 16)

    def arrived(which, target, plane):
        part = target.at[tiles(plane)]
        pltpu.make_async_copy(part, part, recv_sem.at[which, plane]).wait()

    def sent(which, source):
        most = source.at[pl.ds(0, C - 1)]
        pltpu.make_async_copy(most, most, send_sem.at[which]).wait()

    def to_partner(which, buffer, plane):
        part = buffer.at[core, tiles(plane)]
        pltpu.make_async_remote_copy(
            src_ref=part,
            dst_ref=part,
            send_sem=core_send.at[which],
            recv_sem=core_recv.at[which, plane],
            device_id=partner,
            device_id_type=MESH,
        ).start()

    def from_partner(which, buffer, plane):
        part = buffer.at[other, tiles(plane)]
        pltpu.make_async_copy(part, part, core_recv.at[which, plane]).wait()

    def to_partner_sent(which, buffer):
        pltpu.make_async_copy(buffer.at[core], buffer.at[core], core_send.at[which]).wait()

    for load in loads[:4]:
        load.wait()
    wt[...] = w_ref[...].astype(F32).T.astype(BF16)
    in_gain = column(ig_ref)
    in_bias = column(ib_ref)
    for g in range(GROUPS):
        act = x_ref[pl.ds(g * 128, 128), :].astype(F32).T
        shifted = act - jnp.sum(act, axis=0, keepdims=True) * (1.0 / C)
        scale = lax.rsqrt(jnp.sum(shifted * shifted, axis=0, keepdims=True) * (1.0 / C) + EPSILON)
        hat = shifted * scale
        normed[g] = hat
        sinv[g] = jnp.broadcast_to(scale, (8, 128))
        normal[g] = (hat * in_gain + in_bias).astype(BF16)
        projected = nn(wt[pl.ds(256, 256), :], normal[g])
        val, sig = projected[:128], jax.nn.sigmoid(projected[128:])
        factor = sig * val
        right_a[g] = sig
        right_b[g] = factor * (1.0 - sig)
        stage[0, pl.ds(g, C, stride=8), :] = factor
    pl.semaphore_wait(barrier, C)

    def rows(plane):
        return pl.ds(pl.multiple_of(plane * 128, 128), 128)

    def send_factor(which, held, source, target):
        def step(n):
            plane = going_to(n)
            source[tiles(plane)] = stage[held, rows(plane), :].reshape(16, 8, 128).astype(BF16)
            send_plane(which, n, source, target)

        each_plane(step)

    send_factor(RIGHT, 0, r_send, r_all.at[core])

    for g in range(GROUPS):
        projected = nn(wt[pl.ds(0, 256), :], normal[g])
        val, sig = projected[:128], jax.nn.sigmoid(projected[128:])
        factor = sig * val
        left_a[g] = sig
        left_b[g] = factor * (1.0 - sig)
        stage[1, pl.ds(g, C, stride=8), :] = factor
    send_factor(LEFT, 1, l_send, l_all.at[core])

    for load in loads[4:]:
        load.wait()
    owt[...] = ow_ref[...].astype(F32).T.astype(BF16)
    out_gain = column(og_ref)
    mean_h = []
    for g in range(GROUPS):
        out_gate = jax.nn.sigmoid(nn(wt[pl.ds(512, 128), :], normal[g]))
        cotangent = cot_ref[pl.ds(g * 128, 128), :].astype(F32).T
        grad_mixed = cotangent * out_gate
        gate[g] = out_gate
        cot_t[g] = cotangent
        h = nn(ow_ref[...], grad_mixed.astype(BF16)) * out_gain
        hid[pl.ds(g, C, stride=8), :] = h
        mean_h.append(jnp.sum(h, axis=0, keepdims=True) * (1.0 / C))
    mean_h = jnp.concatenate(mean_h, axis=0)

    def place_right(half, plane):
        got = r_all[half, tiles(plane)].astype(F32).reshape(2, 8, 8, 128)
        for pair in range(4):
            even, odd = swap_halves(got[:, 2 * pair], got[:, 2 * pair + 1])
            for high in range(2):
                at = high * 8 + plane
                r_f32[pair, at, pl.ds(half * 16, 8, stride=2), :] = even[high]
                r_f32[pair, at, pl.ds(half * 16 + 1, 8, stride=2), :] = odd[high]

    def right_here(n):
        plane = coming_from(n)
        arrived(RIGHT, r_all.at[core], plane)
        to_partner(0, r_all, plane)
        place_right(core, plane)

    def right_there(n):
        plane = coming_from(n)
        from_partner(0, r_all, plane)
        place_right(other, plane)

    each_plane(right_here)
    each_plane(right_there)
    for pair in range(4):
        part = r_f32[pair].reshape(N, 128)
        r_mat[:, pl.ds(128 * pair, 128)] = part.astype(BF16)
        r_matt[pl.ds(128 * pair, 128), :] = part.T.astype(BF16)

    def place_pairs(buffer, half, plane, matrix):
        got = buffer[half, tiles(plane)].astype(F32).reshape(2, 8, 8, 128)
        parts = []
        for pair in range(4):
            even, odd = swap_halves(got[:, 2 * pair], got[:, 2 * pair + 1])
            parts.append(
                jnp.concatenate([even.reshape(16, 128), odd.reshape(16, 128)], axis=0).astype(BF16)
            )
        whole = jnp.concatenate(parts, axis=1)
        matrix[half, plane] = whole
        return whole

    def take_pieces(even, odd, buffer, plane):
        out = []
        for pair in range(4):
            out.extend(swap_halves(even(pair), odd(pair)))
        whole = jnp.stack(out, axis=1).reshape(16, 8, 128)
        buffer[tiles(plane)] = whole.astype(BF16)

    def take_rows(value, buffer, plane):
        def part(parity):
            return lambda pair: value[
                16 * parity : 16 * parity + 16, 128 * pair : 128 * pair + 128
            ].reshape(2, 8, 128)

        take_pieces(part(0), part(1), buffer, plane)

    def product(n):
        plane = coming_from(n)
        arrived(LEFT, l_all.at[core], plane)
        to_partner(1, l_all, plane)
        whole = place_pairs(l_all, core, plane, l_mat)
        take_rows(nn(whole, r_matt[...]), t_send, plane)

    def mirrored(n):
        return jnp.where(n == 0, 0, jnp.where(n == 7, 7, n + 2 * lax.rem(n, 2) - 1))

    def product_step(n):
        product(n)
        send_plane(TRI, mirrored(n), t_send, t_recv)

    each_plane(product_step)

    def left_there(n):
        plane = coming_from(n)
        from_partner(1, l_all, plane)
        place_pairs(l_all, other, plane, l_mat)

    each_plane(left_there)

    each_plane(lambda n: arrived(TRI, t_recv, coming_from(n)))
    tri = t_recv[...].astype(F32)
    mean_tri = jnp.sum(tri, axis=0) * (1.0 / C)
    shifted = tri - mean_tri[None]
    scale_tri = lax.rsqrt(jnp.sum(shifted * shifted, axis=0) * (1.0 / C) + EPSILON)
    shift[...] = shifted.reshape(C * 8, 128)
    second = jnp.sum(hid[...].reshape(C, 8, 128) * shifted, axis=0) * (scale_tri * (1.0 / C))
    weight = scale_tri * second

    def grad_step(n):
        plane = going_to(n)
        h = hid[rows(plane), :].reshape(16, 8, 128)
        off = shift[rows(plane), :].reshape(16, 8, 128)
        grad_tri = scale_tri[None] * (h - mean_h[None] - off * weight[None])
        g_send[tiles(plane)] = grad_tri.astype(BF16)
        send_plane(GRAD, n, g_send, g_all.at[core])

    each_plane(grad_step)

    out_bias = column(ob_ref)
    for g in range(GROUPS):
        hat = shift[pl.ds(g, C, stride=8), :] * scale_tri[g : g + 1]
        mixed = nn(owt[...], (hat * out_gain + out_bias).astype(BF16))
        out_gate = gate[g]
        grad_logit = cot_t[g] * mixed * out_gate * (1.0 - out_gate)
        grad_acc[g] = nn(w_ref[:, pl.ds(512, 128)], grad_logit.astype(BF16))

    def left_step(n):
        plane = coming_from(n)
        arrived(GRAD, g_all.at[core], plane)
        to_partner(2, g_all, plane)
        whole = place_pairs(g_all, core, plane, gt_mat)
        take_rows(nn(whole, r_mat[...]), gl_send, plane)
        send_plane(GRAD_LEFT, mirrored(n), gl_send, gl_recv)

    each_plane(left_step)

    def grad_there(n):
        plane = coming_from(n)
        from_partner(2, g_all, plane)
        place_pairs(g_all, other, plane, gt_mat)

    def grad_right(half):
        for pair in range(4):
            block = gt_mat[half, :, :, pl.ds(128 * pair, 128)].reshape(256, 128)
            gtt[pl.ds(4 * pair, 4)] = block.astype(F32).T.reshape(4, 32, 256)
        mine = gtt[:, pl.ds(pl.multiple_of(16 * core, 16), 16), :].reshape(256, 256)
        return nn(mine.astype(BF16), l_mat[half].reshape(256, N))

    total = grad_right(core)
    each_plane(grad_there)
    total = total + grad_right(other)
    for pair in range(4):
        gr_f32[pair] = total[:, 128 * pair : 128 * pair + 128].reshape(2, 8, 16, 128)

    def right_step(n):
        plane = going_to(n)

        def part(parity):
            return lambda pair: gr_f32[pair, :, plane, pl.ds(parity, 8, stride=2), :]

        take_pieces(part(0), part(1), gr_send, plane)
        send_plane(GRAD_RIGHT, n, gr_send, gr_recv)

    each_plane(right_step)

    def back(which, buffer, held):
        def step(n):
            plane = coming_from(n)
            arrived(which, buffer, plane)
            stage[held, rows(plane), :] = buffer[tiles(plane)].astype(F32).reshape(128, 128)

        each_plane(step)

    back(GRAD_LEFT, gl_recv, 0)
    for g in range(GROUPS):
        grad = stage[0, pl.ds(g, C, stride=8), :]
        both = jnp.concatenate([grad * left_a[g], grad * left_b[g]], axis=0).astype(BF16)
        grad_acc[g] += nn(w_ref[:, pl.ds(0, 256)], both)

    back(GRAD_RIGHT, gr_recv, 1)
    for g in range(GROUPS):
        grad = stage[1, pl.ds(g, C, stride=8), :]
        both = jnp.concatenate([grad * right_a[g], grad * right_b[g]], axis=0).astype(BF16)
        full = (grad_acc[g] + nn(w_ref[:, pl.ds(256, 256)], both)) * in_gain
        hat = normed[g]
        first = jnp.sum(full, axis=0, keepdims=True) * (1.0 / C)
        second = jnp.sum(full * hat, axis=0, keepdims=True) * (1.0 / C)
        grad_pair = sinv[g][:1] * (full - first - hat * second)
        out_ref[pl.ds(g * 128, 128), :] = grad_pair.T.astype(BF16)

    for which, source in enumerate((r_send, l_send, t_send, g_send, gl_send, gr_send)):
        sent(which, source)
    for which, buffer in enumerate((r_all, l_all, g_all)):
        to_partner_sent(which, buffer)


def on_device(pair_act, cotangent, in_gain, in_bias, proj_weight, out_gain, out_bias, out_weight):
    pairs = pair_act.shape[0] * pair_act.shape[1]
    operands = (
        pair_act.reshape(pairs, C),
        cotangent.reshape(pairs, C),
        in_gain.reshape(1, C),
        in_bias.reshape(1, C),
        proj_weight,
        out_gain.reshape(1, C),
        out_bias.reshape(1, C),
        out_weight,
    )
    pieces = pltpu.VMEM((C, 8, 128), BF16)
    both = pltpu.VMEM((2, C, 8, 128), BF16)
    kept = pltpu.VMEM((GROUPS, C, 128), F32)
    flat = pltpu.VMEM((C * 8, 128), F32)
    out = pl.pallas_call(
        body,
        out_shape=jax.ShapeDtypeStruct((pairs, C), BF16),
        in_specs=[pl.BlockSpec(memory_space=pl.ANY)] * 8,
        out_specs=pl.BlockSpec(memory_space=pltpu.VMEM),
        scratch_shapes=[pltpu.VMEM(a.shape, a.dtype) for a in operands] + [
            pltpu.VMEM((5 * C, C), BF16),
            pltpu.VMEM((C, C), BF16),
            pltpu.VMEM((GROUPS, C, 128), BF16),
            kept,
            pltpu.VMEM((GROUPS, 8, 128), F32),
            kept, kept, kept, kept, kept, kept, kept,
            flat, flat,
            pltpu.VMEM((2, C * 8, 128), F32),
            pieces, both, pieces, both, pieces, pieces, pieces, both,
            pieces, pieces, pieces, pieces,
            pltpu.VMEM((4, 16, 32, 128), F32),
            pltpu.VMEM((N, N), BF16),
            pltpu.VMEM((N, N), BF16),
            pltpu.VMEM((2, PLANES, 32, N), BF16),
            pltpu.VMEM((2, PLANES, 32, N), BF16),
            pltpu.VMEM((16, 32, 256), F32),
            pltpu.VMEM((4, 2, 8, 16, 128), F32),
            pltpu.SemaphoreType.DMA((8,)),
            pltpu.SemaphoreType.DMA((6,)),
            pltpu.SemaphoreType.DMA((6, PLANES)),
            pltpu.SemaphoreType.DMA((3,)),
            pltpu.SemaphoreType.DMA((3, PLANES)),
        ],
        compiler_params=pltpu.CompilerParams(
            collective_id=0, has_side_effects=True, vmem_limit_bytes=60 << 20
        ),
    )(*operands)
    return out.reshape(pair_act.shape)


def solution(mesh):
    placed = (P("row", "ch", None), P("row", "ch", None), P(), P(), P(), P(), P(), P())
    return jax.shard_map(
        on_device, mesh=mesh, in_specs=placed, out_specs=P("row", "ch", None), check_vma=False
    )
```

time: 70.6 us -> 61.8 us (0.88)
  Pallas kernels: 65.3 us -> 60.1 us
  local copies, waits for them, and re-layouts: 4.97 us -> 1.67 us
    pallas_call x1, Pallas kernels: 65.3 us -> 60.1 us  [on_device(): pl.pallas_call(body, out_shape=jax.ShapeDtypeStruct((pairs, C), BF16), in...]
    unnamed x17 -> x1, local copies, waits for them, and re-layouts: 4.97 us -> 1.67 us
where the time goes in v2:
time: 61.8 us; the launch traced here: 61.7 us
  Pallas kernels  60.1 us (97%)
  local copies, waits for them, and re-layouts  1.67 us (3%)
    pallas_call x1, Pallas kernels, on_device(): pl.pallas_call(body, out_shape=jax.ShapeDtypeStruct((pairs, C), BF16), in...  60.1 us
    unnamed x1, local copies, waits for them, and re-layouts  1.67 us

profile of v2, /device:TPU:1, one launch (start us, length us, event | category | flops | bytes accessed | tf_op | source)
XLA Modules:
  0.0 61.7 jit_solution(17754400471025863525)
XLA Ops:
  0.0 60.1 %shard_map.82 = bf16[1024,128]{1,0:T(8,128)(2,1)} custom-call(bf16[1024,128]{1,0:T(8,128)(2,1)} %bitcast.8, bf16[1024,128]{1,0:T(8,128)(2,1)} %bitcast.9, f32[1,128]{1,0:T(1,128)} %bitcast.10, f32[1,128]{1,0:T(1,128)} %bitcast.11, bf16[128,640]{1,0:T(8,128)(2,1)} %w_hbm.1, f32[1,128]{1,0:T(1,128)} %bitcast.12, f32[1,128]{1,0:T(1,128)} %bitcast.13, ...), custom_call_target="tpu_custom_call" | custom-call | tf_op jit(solution)/shard_map/pallas_call | solution.py:411
  60.1 1.7 %copy.10 = bf16[16,64,128]{2,1,0:T(8,128)(2,1)} copy(bf16[16,64,128]{2,1,0:T(8,128)(2,1)} %bitcast.7) | data formatting | bytes 524288

commit v3 on v2

--- a/solution.py
+++ b/solution.py
@@ -14,6 +14,7 @@
 GROUPS = 8
 PLANES = 8
 FAR = (2, 1, 3, 0)
+FAR_PLANES = (4, 3, 5, 2, 6, 1, 7, 0)
 RIGHT, LEFT, TRI, GRAD, GRAD_LEFT, GRAD_RIGHT = range(6)
 
 
@@ -35,7 +36,7 @@
 
 
 def distance(n):
-    return 4 + ((n + 1) // 2) * (1 - 2 * lax.rem(n, 2))
+    return jnp.where(n == 0, 0, 4 + (n // 2) * (2 * lax.rem(n, 2) - 1))
 
 
 def body(
@@ -92,7 +93,7 @@
                 barrier, inc=1, device_id=device(plane, chip), device_id_type=MESH
             )
 
-        @pl.when(n < PLANES - 1)
+        @pl.when(n > 0)
         def _():
             pl.semaphore_signal(
                 barrier, inc=1, device_id=device(plane, chips[-1]), device_id_type=MESH
@@ -116,13 +117,50 @@
         for chip in chips[:-1]:
             send(chip)
 
-        @pl.when(n < PLANES - 1)
+        @pl.when(n > 0)
         def _():
             send(chips[-1])
 
-        @pl.when(n == PLANES - 1)
+        @pl.when(n == 0)
         def _():
             pltpu.make_async_copy(source.at[me], target.at[me], recv_sem.at[which, z]).start()
+
+    zs = [lax.rem(z + d, PLANES) for d in FAR_PLANES]
+
+    def row_base(step):
+        yy = lax.rem(y + 2 + ((step + 1) // 2) * (1 - 2 * lax.rem(step, 2)), 4)
+        return yy // 2, lax.rem(yy, 2) * 4
+
+    def send_row(which, step, source, target):
+        high, low = row_base(step)
+        for dx, xx in zip(FAR, xs):
+            for dz, plane in zip(FAR_PLANES, zs):
+                chip = (high, low + xx)
+
+                def send():
+                    pltpu.make_async_remote_copy(
+                        src_ref=source.at[slot(plane, chip)],
+                        dst_ref=target.at[me],
+                        send_sem=send_sem.at[which],
+                        recv_sem=recv_sem.at[which, z],
+                        device_id=device(plane, chip),
+                        device_id_type=MESH,
+                    ).start()
+
+                if dx or dz:
+                    send()
+                else:
+                    pl.when(step < 3)(send)
+
+                    @pl.when(step == 3)
+                    def _():
+                        own = pltpu.make_async_copy(
+                            source.at[me], target.at[me], recv_sem.at[which, z]
+                        )
+                        own.start()
+
+    def each_row(step):
+        lax.fori_loop(0, 4, lambda n, carry: (step(n), carry)[1], 0)
 
     def going_to(n):
         return lax.rem(z + distance(n), PLANES)
@@ -183,15 +221,23 @@
     def rows(plane):
         return pl.ds(pl.multiple_of(plane * 128, 128), 128)
 
-    def send_factor(which, held, source, target):
-        def step(n):
-            plane = going_to(n)
-            source[tiles(plane)] = stage[held, rows(plane), :].reshape(16, 8, 128).astype(BF16)
-            send_plane(which, n, source, target)
-
-        each_plane(step)
-
-    send_factor(RIGHT, 0, r_send, r_all.at[core])
+    def send_left(n):
+        plane = going_to(n)
+        l_send[tiles(plane)] = stage[1, rows(plane), :].reshape(16, 8, 128).astype(BF16)
+        send_plane(LEFT, n, l_send, l_all.at[core])
+
+    def row_tiles(plane, base):
+        return pl.ds(pl.multiple_of(plane * 16 + base, 4), 4)
+
+    def row_rows(plane, base):
+        return pl.ds(pl.multiple_of((plane * 16 + base) * 8, 32), 32)
+
+    def send_right(n):
+        plane = going_to(n)
+        r_send[tiles(plane)] = stage[0, rows(plane), :].reshape(16, 8, 128).astype(BF16)
+        send_plane(RIGHT, n, r_send, r_all.at[core])
+
+    each_plane(send_right)
 
     for g in range(GROUPS):
         projected = nn(wt[pl.ds(0, 256), :], normal[g])
@@ -200,7 +246,7 @@
         left_a[g] = sig
         left_b[g] = factor * (1.0 - sig)
         stage[1, pl.ds(g, C, stride=8), :] = factor
-    send_factor(LEFT, 1, l_send, l_all.at[core])
+    each_plane(send_left)
 
     for load in loads[4:]:
         load.wait()
@@ -233,13 +279,18 @@
         to_partner(0, r_all, plane)
         place_right(core, plane)
 
-    def right_there(n):
-        plane = coming_from(n)
-        from_partner(0, r_all, plane)
-        place_right(other, plane)
-
     each_plane(right_here)
-    each_plane(right_there)
+    each_plane(lambda n: from_partner(0, r_all, coming_from(n)))
+    for pair in range(4):
+        got = r_all[other].reshape(PLANES, 2, 8, 8, 128)
+        even, odd = swap_halves(
+            got[:, :, 2 * pair].astype(F32).reshape(16, 8, 128),
+            got[:, :, 2 * pair + 1].astype(F32).reshape(16, 8, 128),
+        )
+        for at in range(16):
+            to = (at % 2) * 8 + at // 2
+            r_f32[pair, to, pl.ds(other * 16, 8, stride=2), :] = even[at]
+            r_f32[pair, to, pl.ds(other * 16 + 1, 8, stride=2), :] = odd[at]
     for pair in range(4):
         part = r_f32[pair].reshape(N, 128)
         r_mat[:, pl.ds(128 * pair, 128)] = part.astype(BF16)
@@ -272,28 +323,38 @@
 
         take_pieces(part(0), part(1), buffer, plane)
 
-    def product(n):
-        plane = coming_from(n)
-        arrived(LEFT, l_all.at[core], plane)
-        to_partner(1, l_all, plane)
-        whole = place_pairs(l_all, core, plane, l_mat)
-        take_rows(nn(whole, r_matt[...]), t_send, plane)
-
     def mirrored(n):
-        return jnp.where(n == 0, 0, jnp.where(n == 7, 7, n + 2 * lax.rem(n, 2) - 1))
-
-    def product_step(n):
-        product(n)
-        send_plane(TRI, mirrored(n), t_send, t_recv)
-
-    each_plane(product_step)
-
-    def left_there(n):
-        plane = coming_from(n)
-        from_partner(1, l_all, plane)
-        place_pairs(l_all, other, plane, l_mat)
-
-    each_plane(left_there)
+        return jnp.where(n < 2, n, n + 1 - 2 * lax.rem(n, 2))
+
+    def multiply(got, link, buffer, matrix, factor, replied, send, target):
+        def step(pair, carry):
+            steps = (2 * pair, 2 * pair + 1)
+            planes = [coming_from(n) for n in steps]
+            wholes = []
+            for plane in planes:
+                arrived(got, buffer.at[core], plane)
+                to_partner(link, buffer, plane)
+                wholes.append(place_pairs(buffer, core, plane, matrix))
+            value = nn(jnp.concatenate(wholes, axis=0), factor[...])
+            for i, plane in enumerate(planes):
+                take_rows(value[32 * i : 32 * i + 32], send, plane)
+                send_plane(replied, mirrored(steps[i]), send, target)
+            return carry
+
+        lax.fori_loop(0, PLANES // 2, step, 0)
+
+    def fetch(link, buffer, matrix):
+        each_plane(lambda n: from_partner(link, buffer, coming_from(n)))
+        got = buffer[other].reshape(PLANES, 2, 8, 8, 128)
+        for pair in range(4):
+            even, odd = swap_halves(
+                got[:, :, 2 * pair].astype(F32), got[:, :, 2 * pair + 1].astype(F32)
+            )
+            part = jnp.stack([even, odd], axis=1).reshape(PLANES, 32, 128)
+            matrix[other, :, :, pl.ds(128 * pair, 128)] = part.astype(BF16)
+
+    multiply(LEFT, 1, l_all, l_mat, r_matt, TRI, t_send, t_recv)
+    fetch(1, l_all, l_mat)
 
     each_plane(lambda n: arrived(TRI, t_recv, coming_from(n)))
     tri = t_recv[...].astype(F32)
@@ -322,44 +383,31 @@
         grad_logit = cot_t[g] * mixed * out_gate * (1.0 - out_gate)
         grad_acc[g] = nn(w_ref[:, pl.ds(512, 128)], grad_logit.astype(BF16))
 
-    def left_step(n):
-        plane = coming_from(n)
-        arrived(GRAD, g_all.at[core], plane)
-        to_partner(2, g_all, plane)
-        whole = place_pairs(g_all, core, plane, gt_mat)
-        take_rows(nn(whole, r_mat[...]), gl_send, plane)
-        send_plane(GRAD_LEFT, mirrored(n), gl_send, gl_recv)
-
-    each_plane(left_step)
-
-    def grad_there(n):
-        plane = coming_from(n)
-        from_partner(2, g_all, plane)
-        place_pairs(g_all, other, plane, gt_mat)
-
-    def grad_right(half):
-        for pair in range(4):
-            block = gt_mat[half, :, :, pl.ds(128 * pair, 128)].reshape(256, 128)
-            gtt[pl.ds(4 * pair, 4)] = block.astype(F32).T.reshape(4, 32, 256)
-        mine = gtt[:, pl.ds(pl.multiple_of(16 * core, 16), 16), :].reshape(256, 256)
-        return nn(mine.astype(BF16), l_mat[half].reshape(256, N))
-
-    total = grad_right(core)
-    each_plane(grad_there)
-    total = total + grad_right(other)
+    multiply(GRAD, 2, g_all, gt_mat, r_mat, GRAD_LEFT, gl_send, gl_recv)
+    fetch(2, g_all, gt_mat)
+    for pair in range(4):
+        block = gt_mat[:, :, :, pl.ds(128 * pair, 128)].reshape(N, 128)
+        gtt[pl.ds(4 * pair, 4)] = block.astype(F32).T.reshape(4, 32, N)
+    mine = gtt[:, pl.ds(pl.multiple_of(16 * core, 16), 16), :].reshape(256, N)
+    total = nn(mine.astype(BF16), l_mat[...].reshape(N, N))
     for pair in range(4):
         gr_f32[pair] = total[:, 128 * pair : 128 * pair + 128].reshape(2, 8, 16, 128)
 
-    def right_step(n):
-        plane = going_to(n)
-
-        def part(parity):
-            return lambda pair: gr_f32[pair, :, plane, pl.ds(parity, 8, stride=2), :]
-
-        take_pieces(part(0), part(1), gr_send, plane)
-        send_plane(GRAD_RIGHT, n, gr_send, gr_recv)
-
-    each_plane(right_step)
+    def right_step(step):
+        high, low = row_base(step)
+        for k in range(2):
+            pair = low // 2 + k
+            both = swap_halves(
+                gr_f32[pair, high, :, pl.ds(0, 8, stride=2), :],
+                gr_f32[pair, high, :, pl.ds(1, 8, stride=2), :],
+            )
+            for e in range(2):
+                piece = both[e].astype(BF16)
+                for plane in range(PLANES):
+                    gr_send[plane * 16 + high * 8 + low + 2 * k + e] = piece[plane]
+        send_row(GRAD_RIGHT, step, gr_send, gr_recv)
+
+    each_row(right_step)
 
     def back(which, buffer, held):
         def step(n):
@@ -410,7 +458,7 @@
     flat = pltpu.VMEM((C * 8, 128), F32)
     out = pl.pallas_call(
         body,
-        out_shape=jax.ShapeDtypeStruct((pairs, C), BF16),
+        out_shape=pltpu.VMEM((pairs, C), BF16),
         in_specs=[pl.BlockSpec(memory_space=pl.ANY)] * 8,
         out_specs=pl.BlockSpec(memory_space=pltpu.VMEM),
         scratch_shapes=[pltpu.VMEM(a.shape, a.dtype) for a in operands] + [
@@ -429,7 +477,7 @@
             pltpu.VMEM((N, N), BF16),
             pltpu.VMEM((2, PLANES, 32, N), BF16),
             pltpu.VMEM((2, PLANES, 32, N), BF16),
-            pltpu.VMEM((16, 32, 256), F32),
+            pltpu.VMEM((16, 32, N), F32),
             pltpu.VMEM((4, 2, 8, 16, 128), F32),
             pltpu.SemaphoreType.DMA((8,)),
             pltpu.SemaphoreType.DMA((6,)),
@@ -438,7 +486,7 @@
             pltpu.SemaphoreType.DMA((3, PLANES)),
         ],
         compiler_params=pltpu.CompilerParams(
-            collective_id=0, has_side_effects=True, vmem_limit_bytes=60 << 20
+            collective_id=0, has_side_effects=True, vmem_limit_bytes=56 << 20
         ),
     )(*operands)
     return out.reshape(pair_act.shape)

time: 61.8 us -> 59.9 us (0.969)
  Pallas kernels: 60.1 us -> 59.1 us
  local copies, waits for them, and re-layouts: 1.67 us -> 0.71 us
    pallas_call x1, Pallas kernels: 60.1 us -> 59.1 us  [on_device(): pl.pallas_call(body, out_shape=pltpu.VMEM((pairs, C), BF16), in_specs=[pl...]
    unnamed x1, local copies, waits for them, and re-layouts: 1.67 us -> 0.71 us
where the time goes in v3:
time: 59.9 us; the launch traced here: 59.8 us
  Pallas kernels  59.1 us (99%)
  local copies, waits for them, and re-layouts  0.71 us (1%)
    pallas_call x1, Pallas kernels, on_device(): pl.pallas_call(body, out_shape=pltpu.VMEM((pairs, C), BF16), in_specs=[pl...  59.1 us

profile of v3, /device:TPU:1, one launch (start us, length us, event | category | flops | bytes accessed | tf_op | source)
XLA Modules:
  0.0 59.8 jit_solution(15520495207209513224)
XLA Ops:
  0.0 59.1 %shard_map.82 = bf16[1024,128]{1,0:T(8,128)(2,1)S(1)} custom-call(bf16[1024,128]{1,0:T(8,128)(2,1)} %bitcast.8, bf16[1024,128]{1,0:T(8,128)(2,1)} %bitcast.9, f32[1,128]{1,0:T(1,128)} %bitcast.10, f32[1,128]{1,0:T(1,128)} %bitcast.11, bf16[128,640]{1,0:T(8,128)(2,1)} %w_hbm.1, f32[1,128]{1,0:T(1,128)} %bitcast.12, f32[1,128]{1,0:T(1,128)} %bitcast.13, ...), custom_call_target="tpu_custom_call" | custom-call | tf_op jit(solution)/shard_map/pallas_call | solution.py:459
  59.1 0.7 %copy.10 = bf16[16,64,128]{2,1,0:T(8,128)(2,1)} copy(bf16[16,64,128]{2,1,0:T(8,128)(2,1)S(1)} %bitcast.7) | data formatting | bytes 524288

commit v4 on v3

--- a/solution.py
+++ b/solution.py
@@ -327,8 +327,7 @@
         return jnp.where(n < 2, n, n + 1 - 2 * lax.rem(n, 2))
 
     def multiply(got, link, buffer, matrix, factor, replied, send, target):
-        def step(pair, carry):
-            steps = (2 * pair, 2 * pair + 1)
+        def step(steps):
             planes = [coming_from(n) for n in steps]
             wholes = []
             for plane in planes:
@@ -339,9 +338,9 @@
             for i, plane in enumerate(planes):
                 take_rows(value[32 * i : 32 * i + 32], send, plane)
                 send_plane(replied, mirrored(steps[i]), send, target)
-            return carry
-
-        lax.fori_loop(0, PLANES // 2, step, 0)
+
+        for steps in ((1,), (2, 3), (0, 4, 5), (6, 7)):
+            step(steps)
 
     def fetch(link, buffer, matrix):
         each_plane(lambda n: from_partner(link, buffer, coming_from(n)))
@@ -387,9 +386,9 @@
     fetch(2, g_all, gt_mat)
     for pair in range(4):
         block = gt_mat[:, :, :, pl.ds(128 * pair, 128)].reshape(N, 128)
-        gtt[pl.ds(4 * pair, 4)] = block.astype(F32).T.reshape(4, 32, N)
+        gtt[pl.ds(4 * pair, 4)] = block.T.reshape(4, 32, N)
     mine = gtt[:, pl.ds(pl.multiple_of(16 * core, 16), 16), :].reshape(256, N)
-    total = nn(mine.astype(BF16), l_mat[...].reshape(N, N))
+    total = nn(mine, l_mat[...].reshape(N, N))
     for pair in range(4):
         gr_f32[pair] = total[:, 128 * pair : 128 * pair + 128].reshape(2, 8, 16, 128)
 
@@ -423,6 +422,11 @@
         both = jnp.concatenate([grad * left_a[g], grad * left_b[g]], axis=0).astype(BF16)
         grad_acc[g] += nn(w_ref[:, pl.ds(0, 256)], both)
 
+    for which, source in enumerate((r_send, l_send, t_send, g_send, gl_send)):
+        sent(which, source)
+    for which, buffer in enumerate((r_all, l_all, g_all)):
+        to_partner_sent(which, buffer)
+
     back(GRAD_RIGHT, gr_recv, 1)
     for g in range(GROUPS):
         grad = stage[1, pl.ds(g, C, stride=8), :]
@@ -434,10 +438,7 @@
         grad_pair = sinv[g][:1] * (full - first - hat * second)
         out_ref[pl.ds(g * 128, 128), :] = grad_pair.T.astype(BF16)
 
-    for which, source in enumerate((r_send, l_send, t_send, g_send, gl_send, gr_send)):
-        sent(which, source)
-    for which, buffer in enumerate((r_all, l_all, g_all)):
-        to_partner_sent(which, buffer)
+    sent(GRAD_RIGHT, gr_send)
 
 
 def on_device(pair_act, cotangent, in_gain, in_bias, proj_weight, out_gain, out_bias, out_weight):
@@ -477,7 +478,7 @@
             pltpu.VMEM((N, N), BF16),
             pltpu.VMEM((2, PLANES, 32, N), BF16),
             pltpu.VMEM((2, PLANES, 32, N), BF16),
-            pltpu.VMEM((16, 32, N), F32),
+            pltpu.VMEM((16, 32, N), BF16),
             pltpu.VMEM((4, 2, 8, 16, 128), F32),
             pltpu.SemaphoreType.DMA((8,)),
             pltpu.SemaphoreType.DMA((6,)),

time: 59.9 us -> 59.3 us (0.990)
  Pallas kernels: 59.1 us -> 58.5 us
where the time goes in v4:
time: 59.3 us; the launch traced here: 59.2 us
  Pallas kernels  58.5 us (99%)
  local copies, waits for them, and re-layouts  0.71 us (1%)
    pallas_call x1, Pallas kernels, on_device(): pl.pallas_call(body, out_shape=pltpu.VMEM((pairs, C), BF16), in_specs=[pl...  58.5 us

profile of v4, /device:TPU:1, one launch (start us, length us, event | category | flops | bytes accessed | tf_op | source)
XLA Modules:
  0.0 59.2 jit_solution(1630541255119863011)
XLA Ops:
  0.0 58.5 %shard_map.82 = bf16[1024,128]{1,0:T(8,128)(2,1)S(1)} custom-call(bf16[1024,128]{1,0:T(8,128)(2,1)} %bitcast.8, bf16[1024,128]{1,0:T(8,128)(2,1)} %bitcast.9, f32[1,128]{1,0:T(1,128)} %bitcast.10, f32[1,128]{1,0:T(1,128)} %bitcast.11, bf16[128,640]{1,0:T(8,128)(2,1)} %w_hbm.1, f32[1,128]{1,0:T(1,128)} %bitcast.12, f32[1,128]{1,0:T(1,128)} %bitcast.13, ...), custom_call_target="tpu_custom_call" | custom-call | tf_op jit(solution)/shard_map/pallas_call | solution.py:460
  58.5 0.7 %copy.10 = bf16[16,64,128]{2,1,0:T(8,128)(2,1)} copy(bf16[16,64,128]{2,1,0:T(8,128)(2,1)S(1)} %bitcast.7) | data formatting | bytes 524288

commit v5 on v4

--- a/solution.py
+++ b/solution.py
@@ -15,6 +15,7 @@
 PLANES = 8
 FAR = (2, 1, 3, 0)
 FAR_PLANES = (4, 3, 5, 2, 6, 1, 7, 0)
+FAR_FIRST = (0, 4, 3, 5, 2, 6, 1, 7)
 RIGHT, LEFT, TRI, GRAD, GRAD_LEFT, GRAD_RIGHT = range(6)
 
 
@@ -36,6 +37,8 @@
 
 
 def distance(n):
+    if isinstance(n, int):
+        return FAR_FIRST[n]
     return jnp.where(n == 0, 0, 4 + (n // 2) * (2 * lax.rem(n, 2) - 1))
 
 
@@ -81,7 +84,8 @@
         return plane * 16 + chip[0] * 8 + chip[1]
 
     def each_plane(step):
-        lax.fori_loop(0, PLANES, lambda n, carry: (step(n), carry)[1], 0)
+        for n in range(PLANES):
+            step(n)
 
     barrier = pltpu.get_barrier_semaphore()
     pl.semaphore_signal(barrier, inc=1, device_id=partner, device_id_type=MESH)
@@ -324,10 +328,11 @@
         take_pieces(part(0), part(1), buffer, plane)
 
     def mirrored(n):
-        return jnp.where(n < 2, n, n + 1 - 2 * lax.rem(n, 2))
+        return n if n < 2 else n + 1 - 2 * (n % 2)
 
     def multiply(got, link, buffer, matrix, factor, replied, send, target):
-        def step(steps):
+        def step(pair, carry):
+            steps = (2 * pair, 2 * pair + 1)
             planes = [coming_from(n) for n in steps]
             wholes = []
             for plane in planes:
@@ -338,9 +343,10 @@
             for i, plane in enumerate(planes):
                 take_rows(value[32 * i : 32 * i + 32], send, plane)
                 send_plane(replied, mirrored(steps[i]), send, target)
-
-        for steps in ((1,), (2, 3), (0, 4, 5), (6, 7)):
-            step(steps)
+            return carry
+
+        for k in range(PLANES // 2):
+            step(k, 0)
 
     def fetch(link, buffer, matrix):
         each_plane(lambda n: from_partner(link, buffer, coming_from(n)))

time: 59.3 us -> 59.3 us (level)
  no operation moved by 1% of the time
where the time goes in v5:
time: 59.3 us
  Pallas kernels  58.6 us (99%)
  local copies, waits for them, and re-layouts  0.71 us (1%)
    pallas_call x1, Pallas kernels, on_device(): pl.pallas_call(body, out_shape=pltpu.VMEM((pairs, C), BF16), in_specs=[pl...  58.6 us

profile of v5, /device:TPU:1, one launch (start us, length us, event | category | flops | bytes accessed | tf_op | source)
XLA Modules:
  0.0 59.3 jit_solution(2455463225080184056)
XLA Ops:
  0.0 58.6 %shard_map.82 = bf16[1024,128]{1,0:T(8,128)(2,1)S(1)} custom-call(bf16[1024,128]{1,0:T(8,128)(2,1)} %bitcast.8, bf16[1024,128]{1,0:T(8,128)(2,1)} %bitcast.9, f32[1,128]{1,0:T(1,128)} %bitcast.10, f32[1,128]{1,0:T(1,128)} %bitcast.11, bf16[128,640]{1,0:T(8,128)(2,1)} %w_hbm.1, f32[1,128]{1,0:T(1,128)} %bitcast.12, f32[1,128]{1,0:T(1,128)} %bitcast.13, ...), custom_call_target="tpu_custom_call" | custom-call | tf_op jit(solution)/shard_map/pallas_call | solution.py:466
  58.6 0.7 %copy.10 = bf16[16,64,128]{2,1,0:T(8,128)(2,1)} copy(bf16[16,64,128]{2,1,0:T(8,128)(2,1)S(1)} %bitcast.7) | data formatting | bytes 524288
